TPU v7x, 32 devices: a whole 2x2x4 slice. The times are simulated.
32 devices in a mesh: parts: 2 (over x), pool: 16 (over z, y, core).
Axes of the slice: x: 2, y: 2, z: 4, core: 2. Of those that a mesh axis runs over, the one named last changes fastest.
Arguments:
- queries: bfloat16 [64, 16384], P('parts', 'pool'), parts along dimension 0, as said below
- kv_pages: bfloat16 [512, 128, 2048], P(('parts', 'pool')), parts along dimension 0, may hold values from -6 to 6
- page_table: int32 [64, 8], P('parts'), parts along dimension 0, may hold values from -1 to 255, as said below
- lengths: int32 [64], P('parts'), parts along dimension 0, may hold values from 1 to 1024, as said below
- out_weight: bfloat16 [16384, 16384], P('pool'), may hold values from -0.5 to 0.5
Outputs:
- projected: bfloat16 [64, 16384], P('parts', 'pool'), parts along dimension 0
There are 2 independent parts, one for each index of `parts`. A program takes and returns all parts, laid end to end along the dimension named above; an argument that names none is the same for every part. Nothing has to cross between parts.
Inputs may be any that keep to these rules, and one draw needn't show every extreme that they name: `page_table`: row s holds ceil(lengths[s] / 128) distinct slot numbers followed by -1; no slot is named twice in the table; slot g lies on pool device g // 16. `lengths`: some sequence has exactly 1024 tokens. `queries`: real values; entries of some heads may be large.
All inputs are finite; a program needn't handle non-finite values.
Results may differ from a plain program's by a relative error of at most 0.009.
Values may be sent and summed in bfloat16 or wider, within the bound.
A program may use at most 128 MiB of HBM per device.

v0:
```python
import jax
import jax.numpy as jnp
from jax import lax
from jax.sharding import PartitionSpec as P

HEADS = 128
KV_HEADS = 8
HEAD_DIM = 128


NEG_FILL = -1e30


def shards(queries, kv_pages, page_table, lengths, out_weight):
    slots = kv_pages.shape[0]
    page_len = kv_pages.shape[1]
    kv_width = kv_pages.shape[2] // 2
    seq_count = page_table.shape[0]
    max_pages = page_table.shape[1]
    heads = HEADS
    kv_heads = KV_HEADS
    head_dim = HEAD_DIM
    group = heads // kv_heads
    all_queries = lax.all_gather(queries, "pool", axis=1, tiled=True)
    slot_ids = lax.axis_index("pool") * slots + jnp.arange(slots, dtype=jnp.int32)
    matches = page_table[:, :, None] == slot_ids[None, None, :]
    owned = jnp.any(matches, axis=1)
    owner_hot = owned.T.astype(jnp.float32)
    page_numbers = jnp.arange(max_pages, dtype=jnp.int32)[None, :, None]
    logical = jnp.sum(jnp.where(matches, page_numbers, 0), axis=(0, 1))
    limits = jnp.sum(jnp.where(owned, lengths[:, None], 0), axis=0)
    positions = logical[:, None] * page_len + jnp.arange(page_len, dtype=jnp.int32)[None, :]
    visible = positions < limits[:, None]
    picked = jnp.dot(
        owner_hot.astype(jnp.bfloat16), all_queries, preferred_element_type=jnp.float32
    )
    query_rows = picked.astype(jnp.bfloat16).reshape(slots, kv_heads, group, head_dim)
    key_rows = kv_pages[:, :, :kv_width].reshape(slots, page_len, kv_heads, head_dim)
    value_rows = kv_pages[:, :, kv_width:].reshape(slots, page_len, kv_heads, head_dim)
    scores = jnp.einsum("pkgd,ptkd->pkgt", query_rows, key_rows, preferred_element_type=jnp.float32)
    scores = scores * head_dim ** (-0.5)
    scores = jnp.where(visible[:, None, None, :], scores, NEG_FILL)
    page_max = jnp.max(scores, axis=3).reshape(slots, heads)
    local_max = jnp.max(
        jnp.where(owner_hot[:, :, None] > 0, page_max[:, None, :], NEG_FILL), axis=0
    )
    top = lax.pmax(local_max, "pool")
    page_top = jnp.dot(owner_hot, top, precision=lax.Precision.HIGHEST)
    weights = jnp.exp(scores - page_top.reshape(slots, kv_heads, group)[:, :, :, None])
    page_total = jnp.sum(weights, axis=3).reshape(slots, heads)
    rounded = weights.astype(jnp.bfloat16)
    page_accum = jnp.einsum(
        "pkgt,ptkd->pkgd", rounded, value_rows, preferred_element_type=jnp.float32
    )
    page_total, page_accum = (page_total, page_accum.reshape(slots, heads, head_dim))
    page_accum = page_accum.reshape(slots, heads * head_dim)
    seq_accum = jnp.dot(owner_hot.T, page_accum, precision=lax.Precision.HIGHEST).reshape(
        seq_count, heads, head_dim
    )
    seq_total = jnp.dot(owner_hot.T, page_total, precision=lax.Precision.HIGHEST)
    whole_accum, whole_total = lax.psum((seq_accum, seq_total), "pool")
    own_heads = heads // lax.axis_size("pool")
    head_start = lax.axis_index("pool") * own_heads
    accum_part = lax.dynamic_slice_in_dim(whole_accum, head_start, own_heads, 1)
    total_part = lax.dynamic_slice_in_dim(whole_total, head_start, own_heads, 1)
    attended = (accum_part / total_part[:, :, None]).astype(jnp.bfloat16).reshape(seq_count, -1)
    partial_value = jnp.dot(attended, out_weight, preferred_element_type=jnp.float32)
    return lax.psum_scatter(partial_value, "pool", scatter_dimension=1, tiled=True).astype(
        jnp.bfloat16
    )


def solution(mesh):
    placed = (
        P("parts", "pool"),
        P(("parts", "pool"), None, None),
        P("parts", None),
        P("parts"),
        P("pool", None),
    )
    return jax.shard_map(
        shards, mesh=mesh, in_specs=placed, out_specs=P("parts", "pool"), check_vma=False
    )
```

profile of v0, /device:TPU:0, one launch (start us, length us, event | category | flops | bytes accessed | tf_op | source)
XLA Modules:
  0.0 302.4 jit_solution(502384469892946937)
XLA Ops:
  6.5 0.0 all-gather.2.cloned.1.call-start
  6.5 0.7 all-gather.2.cloned.1.call-update
  7.3 0.0 all-reduce.2.cloned.1.call-start
  7.3 6.1 %fusion.19 = (bf16[16,128,1024]{2,1,0:T(8,128)(2,1)}, bf16[16,128,1024]{2,1,0:T(8,128)(2,1)}) fusion(bf16[16,128,2048]{2,1,0:T(8,128)(2,1)} %param.6), kind=kLoop, calls=%fused_computation.33 | loop fusion | bytes 16777216 | tf_op jit(solution)/shard_map/slice | solution.py:39
  13.4 6.4 %copy.26 = bf16[16,128,1024]{1,2,0:T(8,128)(2,1)} copy(bf16[16,128,1024]{2,1,0:T(8,128)(2,1)} %get-tuple-element.6) | data formatting | bytes 8388608
  19.8 0.0 copy-start
  19.8 0.0 copy-start.1
  19.8 6.4 %copy.27 = bf16[16,128,1024]{1,2,0:T(8,128)(2,1)} copy(bf16[16,128,1024]{2,1,0:T(8,128)(2,1)} %get-tuple-element.5) | data formatting | bytes 8388608
  26.2 0.0 copy-done
  26.2 0.1 compare_reduce_fusion
  26.3 0.0 copy-done.1
  26.3 0.1 select_reduce_fusion.1
  26.4 0.2 fusion.10
  26.6 0.1 add_compare_fusion
  26.7 23.5 %all-gather.2.cloned.1.call-done = bf16[32,16384]{1,0:T(8,128)(2,1)} async-done(((bf16[32,1024]{1,0:T(8,128)(2,1)}), bf16[32,16384]{1,0:T(8,128)(2,1)}) %all-gather.2.cloned.1.call-update) | async-done | bytes 1048592 | tf_op jit(solution)/shard_map/all_gather | solution.py:24
  50.2 1.5 fusion.1
  51.8 0.1 copy.30
  51.9 3.5 %fusion.20 = (f32[16,8,16]{2,1,0:T(8,128)S(1)}, f32[16,8,16,128]{3,2,1,0:T(8,128)S(1)}) fusion(bf16[16,8,16,128]{3,2,1,0:T(8,128)(2,1)S(1)} %bitcast.47, bf16[16,128,8,128]{1,3,2,0:T(8,128)(2,1)} %bitcast.45, pred[16,128]{1,0:T(8,128)(4,1)S(1)} %add_compare_fusion), kind=kOutput, calls=%fused_computation.34 | convolution fusion | flops 67893248 | bytes 5777408 | tf_op jit(solution)/shard_map/pkgd,ptkd->pkgt/dot_general | solution.py:40
  55.3 0.1 broadcast_in_dim.75
  55.4 0.1 select_reduce_fusion
  55.6 0.1 copy.18
  55.7 59.7 %pmax.7 = f32[8,16,32]{2,1,0:T(8,128)S(1)} all-reduce(f32[8,16,32]{2,1,0:T(8,128)S(1)} %bitcast.48), channel_id=1, replica_groups=mesh['parts'=2,'pool'=16] {'pool'}, use_global_device_ids=true, to_apply=%region_5.6 | all-reduce | flops 4096 | bytes 32768 | tf_op jit(solution)/shard_map/pmax | solution.py:47
  115.4 0.3 fusion.17
  115.8 4.5 %fusion.7 = f32[16,8,16,128]{3,2,1,0:T(8,128)S(1)} fusion(bf16[16,128,8,128]{1,3,2,0:T(8,128)(2,1)} %bitcast.44, f32[16,8,16,128]{3,2,1,0:T(8,128)S(1)} %get-tuple-element.8, f32[16,8,16]{2,1,0:T(8,128)S(1)} %copy.19), kind=kOutput, calls=%fused_computation.11 | convolution fusion | flops 67633152 | bytes 6299648 | tf_op jit(solution)/shard_map/pkgt,ptkd->pkgd/dot_general | solution.py:52
  120.3 2.8 fusion.2
  123.1 0.0 all-reduce.2.cloned.1.call-update
  123.1 0.0 reduce-scatter.2.cloned.1.call-start
  123.1 0.7 fusion.5
  123.8 0.1 reshape.71
  123.9 0.3 fusion.21
  124.2 58.5 %psum.15 = f32[32,128]{0,1:T(8,128)S(1)} all-reduce(f32[32,128]{0,1:T(8,128)S(1)} %fusion.21), channel_id=1, replica_groups=mesh['parts'=2,'pool'=16] {'pool'}, use_global_device_ids=true, to_apply=%region_8.9 | all-reduce | flops 4096 | bytes 32768 | tf_op jit(solution)/shard_map/psum | solution.py:61
  182.7 35.7 %all-reduce.2.cloned.1.call-done = f32[32,128,128]{2,0,1:T(8,128)} async-done(((f32[32,128,128]{2,0,1:T(8,128)}), f32[32,128,128]{2,0,1:T(8,128)}) %all-reduce.2.cloned.1.call-update) | async-done | bytes 2097168 | tf_op jit(solution)/shard_map/psum | solution.py:61
  218.4 15.0 %fusion.11 = f32[32,16384]{1,0:T(8,128)} fusion(bf16[1024,16384]{1,0:T(8,128)(2,1)} %param.9, f32[32,8]{0,1:T(8,128)S(1)} %constant_dynamic-slice_fusion, f32[32,128,128]{2,0,1:T(8,128)} %all-reduce.2.cloned.1.call-done, s32[]{:T(128)S(6)} %select_n.24), kind=kOutput, calls=%fused_computation.18 | convolution fusion | flops 1073807360 | bytes 35783684 | tf_op jit(solution)/shard_map/dot_general | solution.py:67
  233.3 0.0 reduce-scatter.2.cloned.1.call-update
  233.4 61.0 %reduce-scatter.2.cloned.1.call-done = f32[32,1024]{1,0:T(8,128)} async-done(((f32[32,16384]{1,0:T(8,128)}), f32[32,1024]{1,0:T(8,128)}) %reduce-scatter.2.cloned.1.call-update) | async-done | bytes 131088 | tf_op jit(solution)/shard_map/reduce_scatter | solution.py:68
  294.3 1.5 convert_element_type.25
  (5 shorter events, 0.1 us)
Async XLA Ops:
  6.5 43.7 %all-gather.2.cloned.1.call-start = ((), (), s32[]{:S(2)}) async-start(), calls=%async_computation.1 | async-start | bytes 1114112 | tf_op jit(solution)/shard_map/all_gather | solution.py:24
  7.3 211.1 %all-reduce.2.cloned.1.call-start = ((), (), s32[]{:S(2)}) async-start(), calls=%async_computation.2 | async-start | bytes 4194304 | tf_op jit(solution)/shard_map/psum | solution.py:61
  19.8 6.4 %copy-start = (s32[32,8]{0,1:T(8,128)S(1)}, s32[32,8]{0,1:T(8,128)}, u32[]{:S(2)}) copy-start(s32[32,8]{0,1:T(8,128)} %param.7) | copy-start | bytes 3076
  19.8 6.5 %copy-start.1 = (s32[32]{0:T(128)S(1)}, s32[32]{0:T(128)}, u32[]{:S(2)}) copy-start(s32[32]{0:T(128)} %param.8) | copy-start | bytes 388
  123.1 171.2 %reduce-scatter.2.cloned.1.call-start = ((), (), s32[]{:S(2)}) async-start(), calls=%async_computation.3 | async-start | bytes 2228224 | tf_op jit(solution)/shard_map/reduce_scatter | solution.py:68
Sparse Core Ops, SparseCore 0:
  9.5 40.6 all-gather.1
  123.2 95.0 all-reduce.1
  233.5 60.8 reduce-scatter.1
where the time goes:
time: 303 us; the launch traced here: 302 us
  waiting for transfers between devices  121 us (40%)
  blocking collectives  118 us (39%)
  matrix products  27.8 us (9%)
  local copies, waits for them, and re-layouts  19.3 us (6%)
  between operations  13.2 us (4%)
    reduce_scatter x1, waiting for transfers between devices, shards(): lax.psum_scatter(partial_value, 'pool', scatter_dimension=1, tiled=True)  61 us
    pmax x1, blocking collectives, shards(): top = lax.pmax(local_max, 'pool')  59.7 us
    psum x1, blocking collectives, shards(): whole_accum, whole_total = lax.psum((seq_accum, seq_total), 'pool')  58.5 us
    psum x1, waiting for transfers between devices, shards(): whole_accum, whole_total = lax.psum((seq_accum, seq_total), 'pool')  35.7 us
    all_gather x1, waiting for transfers between devices, shards(): all_queries = lax.all_gather(queries, 'pool', axis=1, tiled=True)  23.5 us
    dot_general x1, matrix products, shards(): jnp.dot(attended, out_weight, preferred_element_type=jnp.float32)  15 us
    unnamed x7, local copies, waits for them, and re-layouts  12.9 us
    slice x1, local copies, waits for them, and re-layouts, shards(): kv_pages[:, :, kv_width:].reshape(slots, page_len, kv_heads, head_dim)  6.12 us
  transfers between devices with their start and end apart: 3, of which 3 were waited for; matrix products, arithmetic and copies ran while one was open for 7% of the time, Pallas kernels for 0%

commit v1 on v0

v1 whole, which is shorter than its diff:
```python
import functools

import jax
import jax.numpy as jnp
from jax import lax
from jax.experimental import pallas as pl
from jax.experimental.pallas import tpu as pltpu
from jax.sharding import PartitionSpec as P

HEADS = 128
KV_HEADS = 8
HEAD_DIM = 128
GROUP = HEADS // KV_HEADS
NEG = -1e30
F32 = jnp.float32
BF16 = jnp.bfloat16


def grid_of(n):
    chips = n // 2
    outer = 1
    while outer * outer < chips:
        outer *= 2
    return outer, chips // outer


def kernel(
    n, q_ref, kv_hbm, pages_ref, tiled_ref, left_ref, w_hbm, out_ref,
    kv, w, qall, pick, mask, perm, att,
    acc_send, acc_recv, ml_send, ml_recv,
    part1_send, part1_recv, part2_send, part2_recv, part3_send, part3_recv, total,
    kv_sem, w_sem, q_ssem, q_rsem, acc_ssem, acc_rsem, ml_ssem, ml_rsem,
    s1_ssem, s1_rsem, s2_ssem, s2_rsem, s3_ssem, s3_rsem,
):
    A, B = grid_of(n)
    me = lax.axis_index("pool")
    c = lax.rem(me, 2)
    b = lax.rem(me // 2, B)
    a = me // (2 * B)
    slots, page_len = kv.shape[0], kv.shape[1]
    seqs = q_ref.shape[0]
    max_pages = pages_ref.shape[1]
    own_heads = HEADS // n
    padded = max(own_heads, 8)
    owners = n // KV_HEADS
    rows = own_heads * seqs
    cols = w.shape[1] // n

    def index(x, y, z):
        return (lax.rem(x, A) * B + lax.rem(y, B)) * 2 + z

    def remote(src, dst, ssem, rsem, to):
        return pltpu.make_async_remote_copy(
            src_ref=src, dst_ref=dst, send_sem=ssem, recv_sem=rsem,
            device_id={"pool": to}, device_id_type=pl.DeviceIdType.MESH,
        )

    def kv_copy(p):
        return pltpu.make_async_copy(kv_hbm.at[p], kv.at[p], kv_sem.at[p])

    def w_copy(d):
        span = pl.ds(pl.multiple_of(d * cols, 128), cols)
        return pltpu.make_async_copy(w_hbm.at[:, span], w.at[:, span], w_sem.at[d])

    barrier = pltpu.get_barrier_semaphore()
    for step in range(1, n):
        pl.semaphore_signal(
            barrier, inc=1, device_id={"pool": lax.rem(me + step, n)},
            device_id_type=pl.DeviceIdType.MESH,
        )
    for p in range(slots):
        kv_copy(p).start()

    def q_block(i):
        return qall.at[pl.ds(pl.multiple_of(i * rows, 32), rows), :]

    for h in range(own_heads):
        qall[pl.ds(pl.multiple_of(me * rows + h * seqs, 32), seqs), :] = q_ref[
            :, h * HEAD_DIM : (h + 1) * HEAD_DIM
        ]
    pl.semaphore_wait(barrier, n - 1)

    mate = index(a, b, 1 - c)
    sent = []

    def q_send(i, to):
        copy = remote(q_block(i), q_block(i), q_ssem.at[len(sent)], q_rsem.at[i], to)
        copy.start()
        sent.append(copy)

    def q_wait(i):
        remote(q_block(i), q_block(i), q_ssem.at[0], q_rsem.at[i], mate).wait_recv()

    for ra in range(1, A):
        q_send(me, index(a + ra, b, c))
    for rb in range(1, B):
        q_send(me, index(a, b + rb, c))
    q_send(me, mate)
    for d in range(n):
        w_copy(d).start()

    lane = lax.broadcasted_iota(jnp.int32, (max_pages, page_len), 1)
    rowh = lax.broadcasted_iota(jnp.int32, (GROUP, GROUP * seqs), 0)
    laneh = lax.broadcasted_iota(jnp.int32, (GROUP, GROUP * seqs), 1) // seqs
    token = lax.broadcasted_iota(jnp.int32, (GROUP, page_len), 1).astype(F32)

    def build(p, carry):
        hit = tiled_ref[...] == me * slots + p
        owned = jnp.max(jnp.where(hit, 1.0, 0.0), axis=0, keepdims=True)
        place = pl.ds(pl.multiple_of(p * GROUP, GROUP), GROUP)
        pick[place, :] = jnp.where(rowh == laneh, owned, 0.0).astype(BF16)
        left = jnp.where(
            jnp.logical_and(hit[:, :page_len], lane < seqs), left_ref[:, :page_len], 0
        ).astype(F32)
        left = jnp.sum(jnp.sum(left, axis=0, keepdims=True), axis=1, keepdims=True)
        mask[place, :] = jnp.where(token < left, 1.0, 0.0)
        return carry

    lax.fori_loop(0, slots, build, 0)
    count = slots * GROUP
    to_row = lax.broadcasted_iota(jnp.int32, (count, count), 0)
    from_row = lax.broadcasted_iota(jnp.int32, (count, count), 1)
    perm[...] = jnp.where(
        jnp.logical_and(to_row // slots == from_row % GROUP, to_row % slots == from_row // GROUP),
        1.0, 0.0,
    ).astype(BF16)

    for ra in range(1, A):
        i = index(a + ra, b, c)
        q_wait(i)
        for rb in range(1, B):
            q_send(i, index(a, b + rb, c))
        q_send(i, mate)
    for ra in range(A):
        for rb in range(1, B):
            i = index(a + ra, b + rb, c)
            q_wait(i)
            q_send(i, mate)
    for ra in range(A):
        for rb in range(B):
            q_wait(index(a + ra, b + rb, 1 - c))
    for p in range(slots):
        kv_copy(p).wait()

    spread = jnp.where(
        lax.broadcasted_iota(jnp.int32, (slots, 1, 128), 2)
        == lax.rem(me * slots, 128) + lax.broadcasted_iota(jnp.int32, (slots, 1, 128), 0),
        1.0, 0.0,
    )
    block = own_heads * slots

    def acc_copy(o):
        return remote(
            acc_send.at[pl.ds(pl.multiple_of(o * block, 16), block), :], acc_recv.at[me],
            acc_ssem.at[o], acc_rsem.at[me], o,
        )

    def ml_copy(o):
        return remote(ml_send.at[o], ml_recv.at[me], ml_ssem.at[o], ml_rsem.at[me], o)

    ml_send[...] = jnp.zeros_like(ml_send)
    first = me // owners

    def attend(t, carry):
        k = lax.rem(first + t, KV_HEADS)
        at = pl.multiple_of(k * HEAD_DIM, HEAD_DIM)
        mine = qall[pl.ds(pl.multiple_of(k * GROUP * seqs, GROUP * seqs), GROUP * seqs), :]
        query = jnp.dot(pick[...], mine, preferred_element_type=F32).astype(BF16)
        query = query.reshape(slots, GROUP, HEAD_DIM)
        keys = kv[:, :, pl.ds(at, HEAD_DIM)]
        values = kv[:, :, pl.ds(pl.multiple_of(KV_HEADS * HEAD_DIM + at, 128), HEAD_DIM)]
        score = jnp.einsum("phd,ptd->pht", query, keys, preferred_element_type=F32)
        seen = mask[...].reshape(slots, GROUP, page_len)
        score = jnp.where(seen > 0, score * HEAD_DIM**-0.5, NEG)
        top = jnp.max(score, axis=2, keepdims=True)
        weight = jnp.exp(score - top) * seen
        share = jnp.sum(weight, axis=2, keepdims=True)
        acc = jnp.einsum("pht,ptd->phd", weight.astype(BF16), values, preferred_element_type=F32)
        acc = jnp.dot(
            perm[...], acc.reshape(count, HEAD_DIM).astype(BF16), preferred_element_type=F32
        )
        acc_send[pl.ds(pl.multiple_of(k * count, count), count), :] = acc.astype(BF16)
        top = jnp.sum(top * spread, axis=0)
        share = jnp.sum(share * spread, axis=0)
        for j in range(owners):
            o = k * owners + j
            ml_send[o, 0:own_heads, :] = top[j * own_heads : (j + 1) * own_heads]
            ml_send[o, padded : padded + own_heads, :] = share[j * own_heads : (j + 1) * own_heads]

            @pl.when(o != me)
            def _():
                acc_copy(o).start()
                ml_copy(o).start()

        return carry

    lax.fori_loop(0, KV_HEADS, attend, 0)
    acc_recv[me] = acc_send[pl.ds(pl.multiple_of(me * block, 16), block), :]
    ml_recv[me] = ml_send[me]

    for step in range(1, n):
        i = lax.rem(me + step, n)
        remote(acc_recv.at[i], acc_recv.at[i], acc_ssem.at[i], acc_rsem.at[i], i).wait_recv()
        remote(ml_recv.at[i], ml_recv.at[i], ml_ssem.at[i], ml_rsem.at[i], i).wait_recv()

    all_slots = n * slots
    slot_id = lax.broadcasted_iota(jnp.int32, (seqs, all_slots), 1)
    named = jnp.zeros((seqs, all_slots), F32)
    for j in range(max_pages):
        named = jnp.where(pages_ref[:, j : j + 1] == slot_id, 1.0, named)
    per = 128 // slots
    ml_all = jnp.concatenate(
        [jnp.sum(ml_recv[g * per : (g + 1) * per], axis=0) for g in range(n // per)], axis=1
    )
    for h in range(own_heads):
        top_row = ml_all[h : h + 1, :]
        share_row = ml_all[padded + h : padded + h + 1, :]
        top = jnp.max(jnp.where(named > 0, top_row, -3e38), axis=1, keepdims=True)
        scale = jnp.where(named > 0, jnp.exp(jnp.minimum(top_row - top, 0.0)), 0.0).astype(BF16)
        whole = jnp.sum(scale.astype(F32) * share_row, axis=1, keepdims=True)
        acc = acc_recv[:, h * slots : (h + 1) * slots, :].reshape(all_slots, HEAD_DIM)
        acc = jnp.dot(scale, acc, preferred_element_type=F32)
        att[:, h * HEAD_DIM : (h + 1) * HEAD_DIM] = (acc / whole).astype(BF16)

    tile = min(cols, 256)

    def project(d, put):
        w_copy(d).wait()

        def one(j, carry):
            at = pl.ds(pl.multiple_of(d * cols + j * tile, 128), tile)
            put(
                pl.ds(pl.multiple_of(j * tile, 128), tile),
                jnp.dot(att[...], w[:, at], preferred_element_type=F32),
            )
            return carry

        lax.fori_loop(0, cols // tile, one, 0)

    def part1(t):
        return remote(part1_send.at[t], part1_recv.at[t], s1_ssem.at[t], s1_rsem.at[t], mate)

    def part2(ra, rb):
        t = ra * (B - 1) + rb - 1
        return remote(
            part2_send.at[t], part2_recv.at[t], s2_ssem.at[t], s2_rsem.at[t],
            index(a, b + rb, c),
        )

    def part3(ra):
        t = ra - 1
        return remote(
            part3_send.at[t], part3_recv.at[t], s3_ssem.at[t], s3_rsem.at[t],
            index(a + ra, b, c),
        )

    order = [(ra, rb) for rb in list(range(1, B)) + [0] for ra in list(range(1, A)) + [0]]
    for ra, rb in order:
        t = ra * B + rb

        def put(at, value):
            part1_send[t, :, at] = value.astype(BF16)

        project(index(a + ra, b + rb, 1 - c), put)
        part1(t).start()
    for ra, rb in order:
        t = ra * B + rb

        def put(at, value):
            total[:, at] = value

        project(index(a + ra, b + rb, c), put)
        part1(t).wait_recv()
        value = total[...] + part1_recv[t].astype(F32)
        if rb:
            part2_send[ra * (B - 1) + rb - 1] = value.astype(BF16)
            part2(ra, rb).start()
            continue
        for other in range(1, B):
            part2(ra, other).wait_recv()
            value = value + part2_recv[ra * (B - 1) + other - 1].astype(F32)
        if ra:
            part3_send[ra - 1] = value.astype(BF16)
            part3(ra).start()
            continue
        for other in range(1, A):
            part3(other).wait_recv()
            value = value + part3_recv[other - 1].astype(F32)
        out_ref[...] = value.astype(BF16)

    for copy in sent:
        copy.wait_send()
    for step in range(1, n):
        o = lax.rem(me + step, n)
        acc_copy(o).wait_send()
        ml_copy(o).wait_send()
    for ra, rb in order:
        part1(ra * B + rb).wait_send()
        if rb:
            part2(ra, rb).wait_send()
        elif ra:
            part3(ra).wait_send()


def shards(n, queries, kv_pages, page_table, lengths, out_weight):
    slots, page_len, width = kv_pages.shape
    seqs, max_pages = page_table.shape
    A, B = grid_of(n)
    own_heads = HEADS // n
    padded = max(own_heads, 8)
    depth, features = out_weight.shape
    cols = features // n
    block = own_heads * slots
    tiled = jnp.tile(page_table.T, (1, GROUP))
    left = lengths[None, :] - page_len * jnp.arange(max_pages, dtype=jnp.int32)[:, None]
    left = jnp.tile(left, (1, GROUP))
    vmem = pl.BlockSpec(memory_space=pltpu.VMEM)
    hbm = pl.BlockSpec(memory_space=pl.ANY)
    dma = pltpu.SemaphoreType.DMA
    q_sends = (A - 1) + (B - 1) + 1 + (A - 1) * B + A * (B - 1)
    return pl.pallas_call(
        functools.partial(kernel, n),
        out_shape=jax.ShapeDtypeStruct((seqs, cols), BF16),
        in_specs=[vmem, hbm, vmem, vmem, vmem, hbm],
        out_specs=vmem,
        scratch_shapes=[
            pltpu.VMEM((slots, page_len, width), BF16),
            pltpu.VMEM((depth, features), BF16),
            pltpu.VMEM((HEADS * seqs, HEAD_DIM), BF16),
            pltpu.VMEM((slots * GROUP, GROUP * seqs), BF16),
            pltpu.VMEM((slots * GROUP, page_len), F32),
            pltpu.VMEM((slots * GROUP, slots * GROUP), BF16),
            pltpu.VMEM((seqs, depth), BF16),
            pltpu.VMEM((HEADS * slots, HEAD_DIM), BF16),
            pltpu.VMEM((n, block, HEAD_DIM), BF16),
            pltpu.VMEM((n, 2 * padded, 128), F32),
            pltpu.VMEM((n, 2 * padded, 128), F32),
            pltpu.VMEM((A * B, seqs, cols), BF16),
            pltpu.VMEM((A * B, seqs, cols), BF16),
            pltpu.VMEM((A * (B - 1), seqs, cols), BF16),
            pltpu.VMEM((A * (B - 1), seqs, cols), BF16),
            pltpu.VMEM((A - 1, seqs, cols), BF16),
            pltpu.VMEM((A - 1, seqs, cols), BF16),
            pltpu.VMEM((seqs, cols), F32),
            dma((slots,)), dma((n,)), dma((q_sends,)), dma((n,)),
            dma((n,)), dma((n,)), dma((n,)), dma((n,)),
            dma((A * B,)), dma((A * B,)),
            dma((A * (B - 1),)), dma((A * (B - 1),)),
            dma((A - 1,)), dma((A - 1,)),
        ],
        compiler_params=pltpu.CompilerParams(
            collective_id=0, has_side_effects=True, vmem_limit_bytes=60 * 1024 * 1024
        ),
        name="paged_decode",
    )(queries, kv_pages, page_table, tiled, left, out_weight)


def solution(mesh):
    placed = (
        P("parts", "pool"),
        P(("parts", "pool"), None, None),
        P("parts", None),
        P("parts"),
        P("pool", None),
    )
    return jax.shard_map(
        functools.partial(shards, mesh.shape["pool"]), mesh=mesh, in_specs=placed,
        out_specs=P("parts", "pool"), check_vma=False,
    )
```

time: 303 us -> 64.5 us (0.21)
  waiting for transfers between devices: 121 us -> 0 us
  blocking collectives: 118 us -> 0 us
  Pallas kernels: 0 us -> 58.6 us
  matrix products: 27.8 us -> 0 us
  local copies, waits for them, and re-layouts: 19.3 us -> 4.91 us
  between operations: 13.2 us -> 0.01 us
    reduce_scatter x1 -> x0, waiting for transfers between devices: 61 us -> none  [shards(): lax.psum_scatter(partial_value, 'pool', scatter_dimension=1, tiled=True)]
    pmax x1 -> x0, blocking collectives: 59.7 us -> none  [shards(): top = lax.pmax(local_max, 'pool')]
    pallas_call x0 -> x1, Pallas kernels: none -> 58.6 us  [shards(): pl.pallas_call(functools.partial(kernel, n), out_shape=jax.ShapeDtypeStru...]
    psum x1 -> x0, blocking collectives: 58.5 us -> none  [shards(): whole_accum, whole_total = lax.psum((seq_accum, seq_total), 'pool')]
    psum x1 -> x0, waiting for transfers between devices: 35.7 us -> none  [shards(): whole_accum, whole_total = lax.psum((seq_accum, seq_total), 'pool')]
    dot_general x7 -> x0, matrix products: 27.8 us -> none  [the longest x1 15 us: shards(): jnp.dot(attended, out_weight, preferred_element_type=jnp.float32)]
    all_gather x1 -> x0, waiting for transfers between devices: 23.5 us -> none  [shards(): all_queries = lax.all_gather(queries, 'pool', axis=1, tiled=True)]
    unnamed x7 -> x2, local copies, waits for them, and re-layouts: 12.9 us -> 2.84 us
  transfers between devices with their start and end apart: 3 -> 0, of which waited for: 3 -> 0; matrix products, arithmetic and copies ran while one was open for 7% -> 0% of each run, Pallas kernels for 0% -> 0%
where the time goes in v1:
time: 64.5 us; the launch traced here: 64.3 us
  Pallas kernels  58.6 us (91%)
  local copies, waits for them, and re-layouts  4.91 us (8%)
  other arithmetic  0.73 us (1%)
    pallas_call x1, Pallas kernels, shards(): pl.pallas_call(functools.partial(kernel, n), out_shape=jax.ShapeDtypeStru...  58.6 us
    unnamed x2, local copies, waits for them, and re-layouts  2.84 us
    another operation x2, local copies, waits for them, and re-layouts, shards(): tiled = jnp.tile(page_table.T, (1, GROUP))  1.38 us

profile of v1, /device:TPU:0, one launch (start us, length us, event | category | flops | bytes accessed | tf_op | source)
XLA Modules:
  0.0 64.3 jit_solution(17838913502195132642)
XLA Ops:
  0.0 0.7 %broadcast_subtract_fusion = s32[8,32]{1,0:T(8,128)S(1)} fusion(s32[8]{0:T(128)S(1)} %iota_multiply_fusion, s32[32]{0:T(128)} %param.8), kind=kLoop, calls=%fused_computation | loop fusion | flops 256 | bytes 1184 | tf_op jit(solution)/shard_map/sub | solution.py:315
  0.7 1.4 %copy.6.pages_ref = s32[32,8]{1,0:T(8,128)} copy(s32[32,8]{0,1:T(8,128)} %param.7) | data formatting | bytes 2048 | tf_op args[2]
  2.1 0.7 %tile.21.left_ref = s32[8,512]{1,0:T(8,128)} reshape(s32[8,16,32]{2,1,0:T(8,128)S(1)} %tile.20) | data formatting | bytes 32768 | tf_op jit(solution)/shard_map/tile | solution.py:316
  2.8 0.7 %tile.8 = s32[8,16,32]{2,1,0:T(8,128)S(1)} broadcast(s32[8,32]{1,0:T(8,128)} %bitcast.1), dimensions={0,2} | broadcast | bytes 17408 | tf_op jit(solution)/shard_map/tile | solution.py:314
  3.5 0.7 %tile.9.tiled_ref = s32[8,512]{1,0:T(8,128)} reshape(s32[8,16,32]{2,1,0:T(8,128)S(1)} %tile.8) | data formatting | bytes 32768 | tf_op jit(solution)/shard_map/tile | solution.py:314
  4.2 58.6 %paged_decode.1 = bf16[32,1024]{1,0:T(8,128)(2,1)} custom-call(bf16[32,1024]{1,0:T(8,128)(2,1)} %q_ref.1, bf16[16,128,2048]{2,1,0:T(8,128)(2,1)} %kv_hbm.1, s32[32,8]{1,0:T(8,128)} %copy.6.pages_ref, s32[8,512]{1,0:T(8,128)} %tile.9.tiled_ref, s32[8,512]{1,0:T(8,128)} %tile.21.left_ref, bf16[1024,16384]{1,0:T(8,128)(2,1)} %w_hbm.1), custom_call_target="tpu_custom_call" | custom-call | tf_op jit(solution)/shard_map/paged_decode/pallas_call | solution.py:321
  62.8 1.5 %copy.8 = bf16[32,1024]{1,0:T(8,128)(2,1)} copy(bf16[32,1024]{1,0:T(8,128)(2,1)} %paged_decode.1) | data formatting | bytes 131072
  (2 shorter events, 0.0 us)

commit v2 on v1

--- a/solution.py
+++ b/solution.py
@@ -25,10 +25,10 @@
 
 
 def kernel(
-    n, q_ref, kv_hbm, pages_ref, tiled_ref, left_ref, w_hbm, out_ref,
+    n, q_ref, kv_hbm, pages_ref, w_hbm, out_ref,
     kv, w, qall, pick, mask, perm, att,
     acc_send, acc_recv, ml_send, ml_recv,
-    part1_send, part1_recv, part2_send, part2_recv, part3_send, part3_recv, total,
+    part1_send, part1_recv, part2_send, part2_recv, part3_send, part3_recv,
     kv_sem, w_sem, q_ssem, q_rsem, acc_ssem, acc_rsem, ml_ssem, ml_rsem,
     s1_ssem, s1_rsem, s2_ssem, s2_rsem, s3_ssem, s3_rsem,
 ):
@@ -39,7 +39,7 @@
     a = me // (2 * B)
     slots, page_len = kv.shape[0], kv.shape[1]
     seqs = q_ref.shape[0]
-    max_pages = pages_ref.shape[1]
+    max_pages = pages_ref.shape[1] - 1
     own_heads = HEADS // n
     padded = max(own_heads, 8)
     owners = n // KV_HEADS
@@ -99,25 +99,34 @@
     for d in range(n):
         w_copy(d).start()
 
-    lane = lax.broadcasted_iota(jnp.int32, (max_pages, page_len), 1)
-    rowh = lax.broadcasted_iota(jnp.int32, (GROUP, GROUP * seqs), 0)
-    laneh = lax.broadcasted_iota(jnp.int32, (GROUP, GROUP * seqs), 1) // seqs
-    token = lax.broadcasted_iota(jnp.int32, (GROUP, page_len), 1).astype(F32)
-
-    def build(p, carry):
-        hit = tiled_ref[...] == me * slots + p
-        owned = jnp.max(jnp.where(hit, 1.0, 0.0), axis=0, keepdims=True)
-        place = pl.ds(pl.multiple_of(p * GROUP, GROUP), GROUP)
-        pick[place, :] = jnp.where(rowh == laneh, owned, 0.0).astype(BF16)
-        left = jnp.where(
-            jnp.logical_and(hit[:, :page_len], lane < seqs), left_ref[:, :page_len], 0
-        ).astype(F32)
-        left = jnp.sum(jnp.sum(left, axis=0, keepdims=True), axis=1, keepdims=True)
-        mask[place, :] = jnp.where(token < left, 1.0, 0.0)
-        return carry
-
-    lax.fori_loop(0, slots, build, 0)
     count = slots * GROUP
+    lane = lax.broadcasted_iota(jnp.int32, (seqs, 128), 1)
+    named = jnp.zeros((seqs, 128), F32)
+    left = jnp.zeros((seqs, 128), F32)
+    lengths = pages_ref[:, max_pages : max_pages + 1]
+    for j in range(max_pages):
+        hit = jnp.logical_and(pages_ref[:, j : j + 1] - me * slots == lane, lane < slots)
+        named = jnp.where(hit, 1.0, named)
+        seen = jnp.clip(lengths - j * page_len, 0, page_len).astype(F32)
+        left = jnp.where(hit, seen, left)
+    row_slot = jnp.where(
+        lax.broadcasted_iota(jnp.int32, (count, 128), 0) // GROUP
+        == lax.broadcasted_iota(jnp.int32, (count, 128), 1),
+        1.0, 0.0,
+    ).astype(BF16)
+
+    def rows_of(x):
+        return lax.dot_general(
+            row_slot, x.astype(BF16), (((1,), (1,)), ((), ())), preferred_element_type=F32
+        )
+
+    wide = rows_of(jnp.concatenate([named] * GROUP, axis=0))
+    own_lane = lax.broadcasted_iota(jnp.int32, (count, GROUP * seqs), 1) // seqs
+    own_row = lax.broadcasted_iota(jnp.int32, (count, GROUP * seqs), 0) % GROUP
+    pick[...] = jnp.where(own_lane == own_row, wide, 0.0).astype(BF16)
+    left = jnp.broadcast_to(jnp.sum(left, axis=0, keepdims=True), (page_len, 128))
+    token = lax.broadcasted_iota(jnp.int32, (count, page_len), 1).astype(F32)
+    mask[...] = jnp.where(token < rows_of(left), 1.0, 0.0)
     to_row = lax.broadcasted_iota(jnp.int32, (count, count), 0)
     from_row = lax.broadcasted_iota(jnp.int32, (count, count), 1)
     perm[...] = jnp.where(
@@ -125,20 +134,6 @@
         1.0, 0.0,
     ).astype(BF16)
 
-    for ra in range(1, A):
-        i = index(a + ra, b, c)
-        q_wait(i)
-        for rb in range(1, B):
-            q_send(i, index(a, b + rb, c))
-        q_send(i, mate)
-    for ra in range(A):
-        for rb in range(1, B):
-            i = index(a + ra, b + rb, c)
-            q_wait(i)
-            q_send(i, mate)
-    for ra in range(A):
-        for rb in range(B):
-            q_wait(index(a + ra, b + rb, 1 - c))
     for p in range(slots):
         kv_copy(p).wait()
 
@@ -159,10 +154,8 @@
         return remote(ml_send.at[o], ml_recv.at[me], ml_ssem.at[o], ml_rsem.at[me], o)
 
     ml_send[...] = jnp.zeros_like(ml_send)
-    first = me // owners
-
-    def attend(t, carry):
-        k = lax.rem(first + t, KV_HEADS)
+
+    def attend(k):
         at = pl.multiple_of(k * HEAD_DIM, HEAD_DIM)
         mine = qall[pl.ds(pl.multiple_of(k * GROUP * seqs, GROUP * seqs), GROUP * seqs), :]
         query = jnp.dot(pick[...], mine, preferred_element_type=F32).astype(BF16)
@@ -176,25 +169,62 @@
         weight = jnp.exp(score - top) * seen
         share = jnp.sum(weight, axis=2, keepdims=True)
         acc = jnp.einsum("pht,ptd->phd", weight.astype(BF16), values, preferred_element_type=F32)
+        share = jnp.maximum(share, 1e-30)
+        acc = acc * (1.0 / share)
+        top = top + jnp.log(share)
         acc = jnp.dot(
             perm[...], acc.reshape(count, HEAD_DIM).astype(BF16), preferred_element_type=F32
         )
         acc_send[pl.ds(pl.multiple_of(k * count, count), count), :] = acc.astype(BF16)
         top = jnp.sum(top * spread, axis=0)
-        share = jnp.sum(share * spread, axis=0)
         for j in range(owners):
             o = k * owners + j
             ml_send[o, 0:own_heads, :] = top[j * own_heads : (j + 1) * own_heads]
-            ml_send[o, padded : padded + own_heads, :] = share[j * own_heads : (j + 1) * own_heads]
 
             @pl.when(o != me)
             def _():
                 acc_copy(o).start()
                 ml_copy(o).start()
 
-        return carry
-
-    lax.fori_loop(0, KV_HEADS, attend, 0)
+    near = [ra for ra in (1, A - 1) if 0 < ra < A]
+    turns = list(dict.fromkeys(near + list(range(1, A))))
+    chips = n // 2
+
+    def ready(ra, rb):
+        q_wait(index(a + ra, b + rb, 1 - c))
+        if chips == KV_HEADS:
+            attend(index(a + ra, b + rb, 0) // 2)
+
+    ready(0, 0)
+    for rb in range(1, B):
+        i = index(a, b + rb, c)
+        q_wait(i)
+        q_send(i, mate)
+    for rb in range(1, B):
+        ready(0, rb)
+    for ra in turns:
+        i = index(a + ra, b, c)
+        q_wait(i)
+        for rb in range(1, B):
+            q_send(i, index(a, b + rb, c))
+        q_send(i, mate)
+    for ra in turns:
+        ready(ra, 0)
+    for ra in turns:
+        for rb in range(1, B):
+            i = index(a + ra, b + rb, c)
+            q_wait(i)
+            q_send(i, mate)
+    for ra in turns:
+        for rb in range(1, B):
+            ready(ra, rb)
+    if chips != KV_HEADS:
+
+        def one_head(k, carry):
+            attend(k)
+            return carry
+
+        lax.fori_loop(0, KV_HEADS, one_head, 0)
     acc_recv[me] = acc_send[pl.ds(pl.multiple_of(me * block, 16), block), :]
     ml_recv[me] = ml_send[me]
 
@@ -214,28 +244,18 @@
     )
     for h in range(own_heads):
         top_row = ml_all[h : h + 1, :]
-        share_row = ml_all[padded + h : padded + h + 1, :]
         top = jnp.max(jnp.where(named > 0, top_row, -3e38), axis=1, keepdims=True)
         scale = jnp.where(named > 0, jnp.exp(jnp.minimum(top_row - top, 0.0)), 0.0).astype(BF16)
-        whole = jnp.sum(scale.astype(F32) * share_row, axis=1, keepdims=True)
+        whole = jnp.sum(scale.astype(F32), axis=1, keepdims=True)
         acc = acc_recv[:, h * slots : (h + 1) * slots, :].reshape(all_slots, HEAD_DIM)
         acc = jnp.dot(scale, acc, preferred_element_type=F32)
         att[:, h * HEAD_DIM : (h + 1) * HEAD_DIM] = (acc / whole).astype(BF16)
 
-    tile = min(cols, 256)
-
-    def project(d, put):
+
+    def project(d):
         w_copy(d).wait()
-
-        def one(j, carry):
-            at = pl.ds(pl.multiple_of(d * cols + j * tile, 128), tile)
-            put(
-                pl.ds(pl.multiple_of(j * tile, 128), tile),
-                jnp.dot(att[...], w[:, at], preferred_element_type=F32),
-            )
-            return carry
-
-        lax.fori_loop(0, cols // tile, one, 0)
+        at = pl.ds(pl.multiple_of(d * cols, 128), cols)
+        return jnp.dot(att[...], w[:, at], preferred_element_type=F32)
 
     def part1(t):
         return remote(part1_send.at[t], part1_recv.at[t], s1_ssem.at[t], s1_rsem.at[t], mate)
@@ -254,39 +274,43 @@
             index(a + ra, b, c),
         )
 
-    order = [(ra, rb) for rb in list(range(1, B)) + [0] for ra in list(range(1, A)) + [0]]
-    for ra, rb in order:
+    def give(ra, rb):
         t = ra * B + rb
-
-        def put(at, value):
-            part1_send[t, :, at] = value.astype(BF16)
-
-        project(index(a + ra, b + rb, 1 - c), put)
+        part1_send[t] = project(index(a + ra, b + rb, 1 - c)).astype(BF16)
         part1(t).start()
-    for ra, rb in order:
-        t = ra * B + rb
-
-        def put(at, value):
-            total[:, at] = value
-
-        project(index(a + ra, b + rb, c), put)
-        part1(t).wait_recv()
-        value = total[...] + part1_recv[t].astype(F32)
-        if rb:
-            part2_send[ra * (B - 1) + rb - 1] = value.astype(BF16)
-            part2(ra, rb).start()
-            continue
+
+    def keep(ra, rb):
+        value = project(index(a + ra, b + rb, c))
+        part1(ra * B + rb).wait_recv()
+        return value + part1_recv[ra * B + rb].astype(F32)
+
+    def finish(ra):
+        value = keep(ra, 0)
         for other in range(1, B):
             part2(ra, other).wait_recv()
             value = value + part2_recv[ra * (B - 1) + other - 1].astype(F32)
         if ra:
             part3_send[ra - 1] = value.astype(BF16)
             part3(ra).start()
-            continue
+            return
         for other in range(1, A):
             part3(other).wait_recv()
             value = value + part3_recv[other - 1].astype(F32)
         out_ref[...] = value.astype(BF16)
+
+    turns = list(range(1, A)) + [0]
+    before = None
+    for ra in turns:
+        for rb in list(range(1, B)) + [0]:
+            give(ra, rb)
+        for rb in range(1, B):
+            part2_send[ra * (B - 1) + rb - 1] = keep(ra, rb).astype(BF16)
+            part2(ra, rb).start()
+        if before is not None:
+            finish(before)
+        before = ra
+    finish(0)
+    order = [(ra, rb) for ra in range(A) for rb in range(B)]
 
     for copy in sent:
         copy.wait_send()
@@ -311,9 +335,7 @@
     depth, features = out_weight.shape
     cols = features // n
     block = own_heads * slots
-    tiled = jnp.tile(page_table.T, (1, GROUP))
-    left = lengths[None, :] - page_len * jnp.arange(max_pages, dtype=jnp.int32)[:, None]
-    left = jnp.tile(left, (1, GROUP))
+    pages = jnp.concatenate([page_table, lengths[:, None]], axis=1)
     vmem = pl.BlockSpec(memory_space=pltpu.VMEM)
     hbm = pl.BlockSpec(memory_space=pl.ANY)
     dma = pltpu.SemaphoreType.DMA
@@ -321,7 +343,7 @@
     return pl.pallas_call(
         functools.partial(kernel, n),
         out_shape=jax.ShapeDtypeStruct((seqs, cols), BF16),
-        in_specs=[vmem, hbm, vmem, vmem, vmem, hbm],
+        in_specs=[vmem, hbm, vmem, hbm],
         out_specs=vmem,
         scratch_shapes=[
             pltpu.VMEM((slots, page_len, width), BF16),
@@ -333,15 +355,14 @@
             pltpu.VMEM((seqs, depth), BF16),
             pltpu.VMEM((HEADS * slots, HEAD_DIM), BF16),
             pltpu.VMEM((n, block, HEAD_DIM), BF16),
-            pltpu.VMEM((n, 2 * padded, 128), F32),
-            pltpu.VMEM((n, 2 * padded, 128), F32),
+            pltpu.VMEM((n, padded, 128), F32),
+            pltpu.VMEM((n, padded, 128), F32),
             pltpu.VMEM((A * B, seqs, cols), BF16),
             pltpu.VMEM((A * B, seqs, cols), BF16),
             pltpu.VMEM((A * (B - 1), seqs, cols), BF16),
             pltpu.VMEM((A * (B - 1), seqs, cols), BF16),
             pltpu.VMEM((A - 1, seqs, cols), BF16),
             pltpu.VMEM((A - 1, seqs, cols), BF16),
-            pltpu.VMEM((seqs, cols), F32),
             dma((slots,)), dma((n,)), dma((q_sends,)), dma((n,)),
             dma((n,)), dma((n,)), dma((n,)), dma((n,)),
             dma((A * B,)), dma((A * B,)),
@@ -352,7 +373,7 @@
             collective_id=0, has_side_effects=True, vmem_limit_bytes=60 * 1024 * 1024
         ),
         name="paged_decode",
-    )(queries, kv_pages, page_table, tiled, left, out_weight)
+    )(queries, kv_pages, pages, out_weight)
 
 
 def solution(mesh):

time: 64.5 us -> 49.1 us (0.76)
  Pallas kernels: 58.6 us -> 45.2 us
  local copies, waits for them, and re-layouts: 4.91 us -> 2.97 us
    pallas_call x1, Pallas kernels: 58.6 us -> 45.2 us  [shards(): pl.pallas_call(functools.partial(kernel, n), out_shape=jax.ShapeDtypeStru...]
    another operation x4 -> x0, local copies, waits for them, and re-layouts: 2.07 us -> none  [the longest x2 1.38 us: shards(): tiled = jnp.tile(page_table.T, (1, GROUP))]
    broadcast_in_dim x0 -> x1, local copies, waits for them, and re-layouts: none -> 0.74 us  [shards(): pages = jnp.concatenate([page_table, lengths[:, None]], axis=1)]
    sub x1 -> x0, other arithmetic: 0.72 us -> none  [shards(): lengths[None, :]]
    concatenate x0 -> x1, other arithmetic: none -> 0.68 us  [shards(): pages = jnp.concatenate([page_table, lengths[:, None]], axis=1)]
where the time goes in v2:
time: 49.1 us; the launch traced here: 48.9 us
  Pallas kernels  45.2 us (92%)
  local copies, waits for them, and re-layouts  2.97 us (6%)
  other arithmetic  0.68 us (1%)
    pallas_call x1, Pallas kernels, shards(): pl.pallas_call(functools.partial(kernel, n), out_shape=jax.ShapeDtypeStru...  45.2 us
    unnamed x2, local copies, waits for them, and re-layouts  2.23 us

profile of v2, /device:TPU:0, one launch (start us, length us, event | category | flops | bytes accessed | tf_op | source)
XLA Modules:
  0.0 48.9 jit_solution(4825050393650025407)
XLA Ops:
  0.0 0.8 %copy.6 = s32[32,8]{1,0:T(8,128)S(1)} copy(s32[32,8]{0,1:T(8,128)} %param.7) | data formatting | bytes 2048 | tf_op args[2]
  0.8 0.7 %copy.7 = s32[32,1]{1,0:T(8,128)S(1)} copy(s32[32,1]{0,1:T(1,128)} %bitcast.1) | data formatting | bytes 256 | tf_op jit(solution)/shard_map/broadcast_in_dim | solution.py:338
  1.5 0.7 %pad_add_fusion.pages_ref = s32[32,9]{1,0:T(8,128)} fusion(s32[32,1]{1,0:T(8,128)S(1)} %copy.7, s32[32,8]{1,0:T(8,128)S(1)} %copy.6), kind=kLoop, calls=%fused_computation | loop fusion | flops 288 | bytes 2304 | tf_op jit(solution)/shard_map/concatenate | solution.py:338
  2.2 45.2 %paged_decode.1 = bf16[32,1024]{1,0:T(8,128)(2,1)} custom-call(bf16[32,1024]{1,0:T(8,128)(2,1)} %q_ref.1, bf16[16,128,2048]{2,1,0:T(8,128)(2,1)} %kv_hbm.1, s32[32,9]{1,0:T(8,128)} %pad_add_fusion.pages_ref, bf16[1024,16384]{1,0:T(8,128)(2,1)} %w_hbm.1), custom_call_target="tpu_custom_call" | custom-call | tf_op jit(solution)/shard_map/paged_decode/pallas_call | solution.py:343
  47.4 1.5 %copy.9 = bf16[32,1024]{1,0:T(8,128)(2,1)} copy(bf16[32,1024]{1,0:T(8,128)(2,1)} %paged_decode.1) | data formatting | bytes 131072

commit v3 on v2

--- a/solution.py
+++ b/solution.py
@@ -71,8 +71,10 @@
     for p in range(slots):
         kv_copy(p).start()
 
-    def q_block(i):
-        return qall.at[pl.ds(pl.multiple_of(i * rows, 32), rows), :]
+    half = rows // 2
+
+    def q_block(i, f):
+        return qall.at[pl.ds(pl.multiple_of(i * rows + f * half, 16), half), :]
 
     for h in range(own_heads):
         qall[pl.ds(pl.multiple_of(me * rows + h * seqs, 32), seqs), :] = q_ref[
@@ -83,19 +85,22 @@
     mate = index(a, b, 1 - c)
     sent = []
 
-    def q_send(i, to):
-        copy = remote(q_block(i), q_block(i), q_ssem.at[len(sent)], q_rsem.at[i], to)
+    def q_send(i, f, to):
+        copy = remote(
+            q_block(i, f), q_block(i, f), q_ssem.at[len(sent)], q_rsem.at[2 * i + f], to
+        )
         copy.start()
         sent.append(copy)
 
-    def q_wait(i):
-        remote(q_block(i), q_block(i), q_ssem.at[0], q_rsem.at[i], mate).wait_recv()
-
-    for ra in range(1, A):
-        q_send(me, index(a + ra, b, c))
-    for rb in range(1, B):
-        q_send(me, index(a, b + rb, c))
-    q_send(me, mate)
+    def q_wait(i, f):
+        remote(q_block(i, f), q_block(i, f), q_ssem.at[0], q_rsem.at[2 * i + f], mate).wait_recv()
+
+    for f in range(2):
+        for ra in range(1, A):
+            q_send(me, f, index(a + ra, b, c))
+        for rb in range(1, B):
+            q_send(me, f, index(a, b + rb, c))
+        q_send(me, f, mate)
     for d in range(n):
         w_copy(d).start()
 
@@ -191,30 +196,34 @@
     chips = n // 2
 
     def ready(ra, rb):
-        q_wait(index(a + ra, b + rb, 1 - c))
+        for f in range(2):
+            q_wait(index(a + ra, b + rb, 1 - c), f)
         if chips == KV_HEADS:
             attend(index(a + ra, b + rb, 0) // 2)
 
     ready(0, 0)
     for rb in range(1, B):
         i = index(a, b + rb, c)
-        q_wait(i)
-        q_send(i, mate)
+        for f in range(2):
+            q_wait(i, f)
+            q_send(i, f, mate)
     for rb in range(1, B):
         ready(0, rb)
-    for ra in turns:
-        i = index(a + ra, b, c)
-        q_wait(i)
-        for rb in range(1, B):
-            q_send(i, index(a, b + rb, c))
-        q_send(i, mate)
+    for f in range(2):
+        for ra in turns:
+            i = index(a + ra, b, c)
+            q_wait(i, f)
+            for rb in range(1, B):
+                q_send(i, f, index(a, b + rb, c))
+            q_send(i, f, mate)
     for ra in turns:
         ready(ra, 0)
     for ra in turns:
         for rb in range(1, B):
             i = index(a + ra, b + rb, c)
-            q_wait(i)
-            q_send(i, mate)
+            for f in range(2):
+                q_wait(i, f)
+                q_send(i, f, mate)
     for ra in turns:
         for rb in range(1, B):
             ready(ra, rb)
@@ -339,7 +348,7 @@
     vmem = pl.BlockSpec(memory_space=pltpu.VMEM)
     hbm = pl.BlockSpec(memory_space=pl.ANY)
     dma = pltpu.SemaphoreType.DMA
-    q_sends = (A - 1) + (B - 1) + 1 + (A - 1) * B + A * (B - 1)
+    q_sends = 2 * ((A - 1) + (B - 1) + 1 + (A - 1) * B + A * (B - 1))
     return pl.pallas_call(
         functools.partial(kernel, n),
         out_shape=jax.ShapeDtypeStruct((seqs, cols), BF16),
@@ -363,7 +372,7 @@
             pltpu.VMEM((A * (B - 1), seqs, cols), BF16),
             pltpu.VMEM((A - 1, seqs, cols), BF16),
             pltpu.VMEM((A - 1, seqs, cols), BF16),
-            dma((slots,)), dma((n,)), dma((q_sends,)), dma((n,)),
+            dma((slots,)), dma((n,)), dma((q_sends,)), dma((2 * n,)),
             dma((n,)), dma((n,)), dma((n,)), dma((n,)),
             dma((A * B,)), dma((A * B,)),
             dma((A * (B - 1),)), dma((A * (B - 1),)),

time: 49.1 us -> 50.5 us (1.029)
  Pallas kernels: 45.2 us -> 46.6 us
    pallas_call x1, Pallas kernels: 45.2 us -> 46.6 us  [shards(): pl.pallas_call(functools.partial(kernel, n), out_shape=jax.ShapeDtypeStru...]
where the time goes in v3:
time: 50.5 us; the launch traced here: 50.2 us
  Pallas kernels  46.6 us (92%)
  local copies, waits for them, and re-layouts  2.97 us (6%)
  other arithmetic  0.68 us (1%)
    pallas_call x1, Pallas kernels, shards(): pl.pallas_call(functools.partial(kernel, n), out_shape=jax.ShapeDtypeStru...  46.6 us
    unnamed x2, local copies, waits for them, and re-layouts  2.23 us

profile of v3, /device:TPU:0, one launch (start us, length us, event | category | flops | bytes accessed | tf_op | source)
XLA Modules:
  0.0 50.2 jit_solution(5659103816698583191)
XLA Ops:
  0.0 0.8 %copy.6 = s32[32,8]{1,0:T(8,128)S(1)} copy(s32[32,8]{0,1:T(8,128)} %param.7) | data formatting | bytes 2048 | tf_op args[2]
  0.8 0.7 %copy.7 = s32[32,1]{1,0:T(8,128)S(1)} copy(s32[32,1]{0,1:T(1,128)} %bitcast.1) | data formatting | bytes 256 | tf_op jit(solution)/shard_map/broadcast_in_dim | solution.py:347
  1.5 0.7 %pad_add_fusion.pages_ref = s32[32,9]{1,0:T(8,128)} fusion(s32[32,1]{1,0:T(8,128)S(1)} %copy.7, s32[32,8]{1,0:T(8,128)S(1)} %copy.6), kind=kLoop, calls=%fused_computation | loop fusion | flops 288 | bytes 2304 | tf_op jit(solution)/shard_map/concatenate | solution.py:347
  2.2 46.6 %paged_decode.1 = bf16[32,1024]{1,0:T(8,128)(2,1)} custom-call(bf16[32,1024]{1,0:T(8,128)(2,1)} %q_ref.1, bf16[16,128,2048]{2,1,0:T(8,128)(2,1)} %kv_hbm.1, s32[32,9]{1,0:T(8,128)} %pad_add_fusion.pages_ref, bf16[1024,16384]{1,0:T(8,128)(2,1)} %w_hbm.1), custom_call_target="tpu_custom_call" | custom-call | tf_op jit(solution)/shard_map/paged_decode/pallas_call | solution.py:352
  48.7 1.5 %copy.9 = bf16[32,1024]{1,0:T(8,128)(2,1)} copy(bf16[32,1024]{1,0:T(8,128)(2,1)} %paged_decode.1) | data formatting | bytes 131072
